TPU v7x, 32 devices: a whole 2x2x4 slice. The times are simulated.
32 devices in a mesh: study: 2 (over y), zslab: 4 (over x, core), frame: 4 (over z).
Axes of the slice: x: 2, y: 2, z: 4, core: 2. Of those that a mesh axis runs over, the one named last changes fastest.
Arguments:
- alpha: float32 [32, 64, 2048], P(('study', 'frame'), 'zslab'), parts along dimension 0, may hold values from 0.2 to 2
- measured: float32 [32, 64, 2048], P(('study', 'frame'), 'zslab'), parts along dimension 0, may hold values from 2 to 20
- background: float32 [32, 64, 2048], P(('study', 'frame'), 'zslab'), parts along dimension 0, may hold values from 1 to 4
- norm_image: float32 [32, 64, 2048], P(('study', 'frame'), 'zslab'), parts along dimension 0, may hold values from 3 to 12
- temporal: float32 [16, 16], replicated
- axial: float32 [64, 64], replicated, may hold values from 0 to 3.2, as said below
- kernel: bfloat16 [6144, 128, 128], P(('study', 'zslab', 'frame')), parts along dimension 0
- rows: int32 [6144], P(('study', 'zslab', 'frame')), parts along dimension 0, may hold values from 0 to 1023, as said below
- cols: int32 [6144], P(('study', 'zslab', 'frame')), parts along dimension 0, may hold values from 0 to 1023, as said below
- counts: int32 [32], P(('study', 'zslab', 'frame')), parts along dimension 0, may hold values from 64 to 192, as said below
Outputs:
- alpha_next: float32 [32, 64, 2048], P(('study', 'frame'), 'zslab'), parts along dimension 0
There are 2 independent parts, one for each index of `study`. A program takes and returns all parts, laid end to end along the dimension named above; an argument that names none is the same for every part. Nothing has to cross between parts.
Inputs may be any that keep to these rules, and one draw needn't show every extreme that they name: Slots come in aligned runs of 192, one run for each device of zslab+frame in order, zslab slowest. A block row is plane * 16 + transaxial block; the rows of run d lie in the planes d // 4 * 16 to that + 15 and the transaxial blocks d % 4 * 4 to that + 3, appear in increasing order, and each of them has 1 to 3 live slots. `cols`: A live slot's column block has the transaxial block of its row and a plane at most one away from the row's plane. Slots that are not live repeat the run's first block row as row and column. counts[d] is the number of live slots of run d; they are the first slots of the run. In every draw one run is full. axial[z, y] is zero where |z - y| > 8.
All inputs are finite; a program needn't handle non-finite values.
Results may differ from a plain program's by a relative error of at most 0.0011.
Values may be sent and summed in bfloat16 or wider, within the bound.
A program may use at most 64 MiB of HBM per device.

v0:
```python
import jax
import jax.numpy as jnp
from jax import lax
from jax.sharding import PartitionSpec as P

EXACT = lax.Precision.HIGHEST


def with_halo(cells, sides, width):
    for axis, dim in sides:
        count = lax.axis_size(axis)
        ends = count - 1
        head = lax.slice_in_dim(cells, 0, width, axis=dim)
        tail = lax.slice_in_dim(cells, cells.shape[dim] - width, cells.shape[dim], axis=dim)
        cells = jnp.concatenate(
            [
                lax.ppermute(tail, axis, [(i, (i + 1) % count) for i in range(ends)]),
                cells,
                lax.ppermute(head, axis, [((i + 1) % count, i) for i in range(ends)]),
            ],
            axis=dim,
        )
    return cells


def to_frame_layout(blocked):
    return lax.all_to_all(blocked, "frame", split_axis=0, concat_axis=2, tiled=True)


def on_device(alpha, measured, background, norm_image, temporal, axial, kernel, rows, cols, counts):
    own_frames, planes, row_width = alpha.shape
    block_edge = kernel.shape[1]
    tiles_all = row_width // block_edge
    tile_count = tiles_all // lax.axis_size("frame")
    tile_width = tile_count * block_edge
    slab_index = lax.axis_index("zslab")
    tile_index = lax.axis_index("frame")
    slot_count = kernel.shape[0]
    first_plane = slab_index * planes
    local_rows = (
        (rows // tiles_all - first_plane) * tile_count + rows % tiles_all - tile_index * tile_count
    )
    local_cols = (
        (cols // tiles_all - first_plane + 1) * tile_count
        + cols % tiles_all
        - tile_index * tile_count
    )
    weights = (jnp.arange(slot_count, dtype=jnp.int32) < counts[0]).astype(jnp.float32)
    row_hot = (
        local_rows[None, :] == jnp.arange(planes * tile_count, dtype=jnp.int32)[:, None]
    ).astype(jnp.float32)
    row_hot = row_hot * weights[None, :]
    col_hot = (
        local_cols[None, :] == jnp.arange((planes + 2) * tile_count, dtype=jnp.int32)[:, None]
    ).astype(jnp.float32)
    col_hot = col_hot * weights[None, :]
    lowered = alpha.astype(jnp.bfloat16)
    blocked = lax.all_to_all(lowered, "frame", split_axis=2, concat_axis=0, tiled=True)
    frames = blocked.shape[0]
    extended = with_halo(blocked, (("zslab", 1),), 1)
    ext_blocks = extended.reshape(frames, (planes + 2) * tile_count, block_edge)
    picked = jnp.take(ext_blocks, local_cols, axis=1)
    products = jnp.einsum("smn,fsn->sfm", kernel, picked, preferred_element_type=jnp.float32)
    coef_image = jnp.einsum("rs,sfm->frm", row_hot, products, precision=EXACT).reshape(
        frames, planes, tile_width
    )
    frame_image = jnp.einsum("fg,gzp->fzp", temporal, coef_image, precision=EXACT)
    image_frames = to_frame_layout(frame_image)
    columns, measured_cols, background_cols = (
        lax.all_to_all(image_frames, "zslab", split_axis=2, concat_axis=1, tiled=True),
        lax.all_to_all(measured, "zslab", split_axis=2, concat_axis=1, tiled=True),
        lax.all_to_all(background, "zslab", split_axis=2, concat_axis=1, tiled=True),
    )
    expected = jnp.einsum("zy,fyp->fzp", axial, columns, precision=EXACT) + background_cols
    ratios = measured_cols / expected
    back_cols = jnp.einsum("zy,fzp->fyp", axial, ratios, precision=EXACT)
    back_planes = lax.all_to_all(back_cols, "zslab", split_axis=1, concat_axis=2, tiled=True)
    back_blocks = lax.all_to_all(back_planes, "frame", split_axis=2, concat_axis=0, tiled=True)
    back_frames = jnp.einsum("fg,fzp->gzp", temporal, back_blocks, precision=EXACT)
    back_low = back_frames.astype(jnp.bfloat16).reshape(frames, planes * tile_count, block_edge)
    gathered = jnp.take(back_low, local_rows, axis=1)
    spread_back = jnp.einsum("smn,fsm->sfn", kernel, gathered, preferred_element_type=jnp.float32)
    back_ext = jnp.einsum("cs,sfn->fcn", col_hot, spread_back, precision=EXACT).reshape(
        frames, planes + 2, tile_width
    )
    rim_terms = jnp.concatenate((back_ext[:, :1], back_ext[:, planes + 1 :]), axis=1)
    margins = with_halo(rim_terms, (("zslab", 1),), 1)
    back_coef = back_ext[:, 1 : planes + 1]
    back_coef = back_coef.at[:, 0].add(margins[:, 0])
    back_coef = back_coef.at[:, planes - 1].add(margins[:, 3])
    back_own = to_frame_layout(back_coef)
    return alpha * back_own / norm_image


def solution(mesh):
    placed = (
        P(("study", "frame"), "zslab", None),
        P(("study", "frame"), "zslab", None),
        P(("study", "frame"), "zslab", None),
        P(("study", "frame"), "zslab", None),
        P(),
        P(),
        P(("study", "zslab", "frame"), None, None),
        P(("study", "zslab", "frame")),
        P(("study", "zslab", "frame")),
        P(("study", "zslab", "frame")),
    )
    return jax.shard_map(
        on_device,
        mesh=mesh,
        in_specs=placed,
        out_specs=P(("study", "frame"), "zslab", None),
        check_vma=False,
    )
```

profile of v0, /device:TPU:0, one launch (start us, length us, event | category | flops | bytes accessed | tf_op | source)
XLA Modules:
  0.0 194.9 jit_solution(951847665050092330)
XLA Ops:
  5.4 6.3 %all-to-all-start.1 = ((bf16[4,2,16384]{2,1,0:T(2,128)(2,1)}), bf16[4,2,16384]{2,1,0:T(2,128)(2,1)S(1)}, u32[]{:S(2)}, u32[]{:S(2)}) async-start(bf16[4,2,16384]{2,1,0:T(2,128)(2,1)} %reshape.119), calls=%async_computation.1 | async-start | bytes 524288 | tf_op jit(solution)/shard_map/all_to_all | solution.py:58
  15.4 5.7 %reshape.115 = f32[4,1,32768]{2,1,0:T(1,128)} reshape(f32[2048,4,16]{2,1,0:T(4,128)} %bitcast.102) | data formatting | bytes 1048576
  21.2 3.5 %all-to-all-start = ((f32[4,1,32768]{2,1,0:T(1,128)}), f32[4,1,32768]{2,1,0:T(1,128)S(1)}, u32[]{:S(2)}, u32[]{:S(2)}) async-start(f32[4,1,32768]{2,1,0:T(1,128)} %reshape.115), calls=%async_computation | async-start | bytes 1048576 | tf_op jit(solution)/shard_map/all_to_all | solution.py:71
  35.2 5.5 %fusion.15 = f32[192,16,128]{2,1,0:T(8,128)S(1)} fusion(bf16[192,128,128]{2,1,0:T(8,128)(2,1)} %param.20, bf16[192,16,128]{2,1,0:T(8,128)(2,1)S(1)} %gather_fusion, pred[192]{0:T(512)(128)(4,1)S(1)} %get-tuple-element.31), kind=kOutput, calls=%fused_computation.17 | convolution fusion | flops 101056512 | bytes 8650944 | tf_op jit(solution)/shard_map/smn,fsn->sfm/dot_general | solution.py:63
  44.3 5.1 %all-to-all-start.2 = ((f32[16,16,512]{2,1,0:T(8,128)}), f32[16,16,512]{2,1,0:T(8,128)S(1)}, u32[]{:S(2)}, u32[]{:S(2)}) async-start(f32[16,16,512]{2,1,0:T(8,128)} %copy.78), calls=%async_computation.2 | async-start | bytes 1048576 | tf_op jit(solution)/shard_map/all_to_all | solution.py:27
  52.5 5.7 %reshape.117 = f32[4,1,32768]{2,1,0:T(1,128)} reshape(f32[2048,4,16]{2,1,0:T(4,128)} %bitcast.103) | data formatting | bytes 1048576
  58.2 6.0 %all-to-all-done.2 = f32[16,16,512]{2,1,0:T(8,128)S(1)} async-done(((f32[16,16,512]{2,1,0:T(8,128)}), f32[16,16,512]{2,1,0:T(8,128)S(1)}, u32[]{:S(2)}, u32[]{:S(2)}) %all-to-all-start.2) | async-done | bytes 524320 | tf_op jit(solution)/shard_map/all_to_all | solution.py:27
  64.3 3.5 %all-to-all-start.4 = ((f32[4,1,32768]{2,1,0:T(1,128)}), f32[4,1,32768]{2,1,0:T(1,128)S(1)}, u32[]{:S(2)}, u32[]{:S(2)}) async-start(f32[4,1,32768]{2,1,0:T(1,128)} %reshape.117), calls=%async_computation.4 | async-start | bytes 1048576 | tf_op jit(solution)/shard_map/all_to_all | solution.py:72
  70.8 5.7 %reshape.121 = f32[4,1,32768]{2,1,0:T(1,128)} reshape(f32[2048,4,16]{2,1,0:T(4,128)} %bitcast.96) | data formatting | bytes 1048576
  76.6 3.7 %all-to-all-start.3 = ((f32[4,1,32768]{2,1,0:T(1,128)}), f32[4,1,32768]{2,1,0:T(1,128)S(1)}, u32[]{:S(2)}, u32[]{:S(2)}) async-start(f32[4,1,32768]{2,1,0:T(1,128)} %reshape.121), calls=%async_computation.3 | async-start | bytes 1048576 | tf_op jit(solution)/shard_map/all_to_all | solution.py:70
  82.9 4.9 %reshape.116 = f32[2048,4,16]{2,1,0:T(4,128)} reshape(f32[4,32768]{1,0:T(4,128)S(1)} %reduce.4) | data formatting | bytes 1048576
  87.8 3.4 %copy.71 = f32[4,16,4,512]{3,1,2,0:T(8,128)S(1)} copy(f32[4,16,4,512]{1,0,3,2:T(4,128)} %bitcast.97) | data formatting | bytes 1048576 | tf_op jit(solution)/shard_map/all_to_all | solution.py:71
  93.4 4.9 %reshape.118 = f32[2048,4,16]{2,1,0:T(4,128)} reshape(f32[4,32768]{1,0:T(4,128)S(1)} %reduce.5) | data formatting | bytes 1048576
  98.3 3.7 %copy.84 = f32[4,16,4,512]{3,1,2,0:T(8,128)S(1)} copy(f32[4,16,4,512]{1,0,3,2:T(4,128)} %bitcast.98) | data formatting | bytes 1048576 | tf_op jit(solution)/shard_map/all_to_all | solution.py:72
  104.1 4.9 %reshape.122 = f32[2048,4,16]{2,1,0:T(4,128)} reshape(f32[4,32768]{1,0:T(4,128)S(1)} %reduce.6) | data formatting | bytes 1048576
  109.1 3.4 %copy.82 = f32[4,4,16,512]{3,2,1,0:T(8,128)S(1)} copy(f32[4,4,16,512]{2,0,3,1:T(4,128)} %bitcast.99) | data formatting | bytes 1048576 | tf_op jit(solution)/shard_map/all_to_all | solution.py:70
  114.2 11.9 %all_to_all.144 = f32[4,64,512]{2,0,1:T(4,128)S(1)} all-to-all(f32[4,64,512]{2,0,1:T(4,128)S(1)} %copy.86), channel_id=1, replica_groups=mesh['study'=2,'zslab'=4,'frame'=4] {'zslab'}, dimensions={1} | all-to-all | bytes 1048576 | tf_op jit(solution)/shard_map/all_to_all | solution.py:77
  129.1 5.7 %reshape.123 = f32[4,1,32768]{2,1,0:T(1,128)} reshape(f32[2048,4,16]{2,1,0:T(4,128)} %bitcast.100) | data formatting | bytes 1048576
  134.9 3.7 %all-to-all-start.6 = ((f32[4,1,32768]{2,1,0:T(1,128)}), f32[4,1,32768]{2,1,0:T(1,128)S(1)}, u32[]{:S(2)}, u32[]{:S(2)}) async-start(f32[4,1,32768]{2,1,0:T(1,128)} %reshape.123), calls=%async_computation.6 | async-start | bytes 1048576 | tf_op jit(solution)/shard_map/all_to_all | solution.py:78
  138.7 14.1 %all-to-all-done.6 = f32[4,1,32768]{2,1,0:T(1,128)S(1)} async-done(((f32[4,1,32768]{2,1,0:T(1,128)}), f32[4,1,32768]{2,1,0:T(1,128)S(1)}, u32[]{:S(2)}, u32[]{:S(2)}) %all-to-all-start.6) | async-done | bytes 524320 | tf_op jit(solution)/shard_map/all_to_all | solution.py:78
  154.9 4.9 %reshape.124 = f32[2048,4,16]{2,1,0:T(4,128)} reshape(f32[4,32768]{1,0:T(4,128)S(1)} %reduce.7) | data formatting | bytes 1048576
  159.8 3.5 %copy.90 = f32[4,4,16,512]{3,1,0,2:T(4,128)S(1)} copy(f32[4,4,16,512]{2,1,3,0:T(4,128)} %bitcast.101) | data formatting | bytes 1048576 | tf_op jit(solution)/shard_map/all_to_all | solution.py:78
  165.4 3.9 %fusion.13 = f32[192,16,128]{2,1,0:T(8,128)S(1)} fusion(bf16[192,128,128]{2,1,0:T(8,128)(2,1)} %param.20, bf16[192,16,128]{2,1,0:T(8,128)(2,1)S(1)} %gather_fusion.1, pred[192]{0:T(512)(128)(4,1)S(1)} %get-tuple-element.37), kind=kOutput, calls=%fused_computation.15 | convolution fusion | flops 101056512 | bytes 8650944 | tf_op jit(solution)/shard_map/smn,fsm->sfn/dot_general | solution.py:82
  176.8 17.2 %all_to_all.145 = f32[16,16,512]{2,1,0:T(8,128)S(1)} all-to-all(f32[16,16,512]{2,1,0:T(8,128)S(1)} %scatter-add.9), channel_id=1, replica_groups=mesh['study'=2,'zslab'=4,'frame'=4] {'frame'}, dimensions={0} | all-to-all | bytes 1048576 | tf_op jit(solution)/shard_map/all_to_all | solution.py:27
  (76 shorter events, 52.7 us)
Async XLA Ops:
  0.0 112.5 %copy-start = (f32[64,64]{1,0:T(8,128)S(1)}, f32[64,64]{1,0:T(8,128)}, u32[]{:S(2)}) copy-start(f32[64,64]{1,0:T(8,128)} %param.19) | copy-start | bytes 49156
  0.0 11.7 %copy-start.7 = (s32[192]{0:T(256)S(1)}, s32[192]{0:T(256)}, u32[]{:S(2)}) copy-start(s32[192]{0:T(256)} %param.21) | copy-start | bytes 2308
  0.0 11.7 %copy-start.6 = (s32[192]{0:T(256)S(1)}, s32[192]{0:T(256)}, u32[]{:S(2)}) copy-start(s32[192]{0:T(256)} %param.22) | copy-start | bytes 2308
  0.0 12.4 %copy-start.2 = (f32[4,16,2048]{2,1,0:T(8,128)S(1)}, f32[4,16,2048]{2,1,0:T(8,128)}, u32[]{:S(2)}) copy-start(f32[4,16,2048]{2,1,0:T(8,128)} %param.15) | copy-start | bytes 1572868
  5.4 15.8 %all-to-all-start.1 = ((bf16[4,2,16384]{2,1,0:T(2,128)(2,1)}), bf16[4,2,16384]{2,1,0:T(2,128)(2,1)S(1)}, u32[]{:S(2)}, u32[]{:S(2)}) async-start(bf16[4,2,16384]{2,1,0:T(2,128)(2,1)} %reshape.119), calls=%async_computation.1 | async-start | bytes 524288 | tf_op jit(solution)/shard_map/all_to_all | solution.py:58
  21.2 23.1 %all-to-all-start = ((f32[4,1,32768]{2,1,0:T(1,128)}), f32[4,1,32768]{2,1,0:T(1,128)S(1)}, u32[]{:S(2)}, u32[]{:S(2)}) async-start(f32[4,1,32768]{2,1,0:T(1,128)} %reshape.115), calls=%async_computation | async-start | bytes 1048576 | tf_op jit(solution)/shard_map/all_to_all | solution.py:71
  27.4 3.7 %collective-permute-start = (bf16[16,1,512]{2,1,0:T(2,128)(2,1)S(1)}, bf16[16,1,512]{2,1,0:T(2,128)(2,1)S(1)}, u32[]{:S(2)}, u32[]{:S(2)}) collective-permute-start(bf16[16,1,512]{2,1,0:T(2,128)(2,1)S(1)} %get-tuple-element.35), channel_id=1, source_target_pairs={{0,4},{4,8},{8,12},{1,5},{5,9},{9,13},{2,6},{6,10},{10,14},{3,7},{... | collective-permute-start | bytes 49160 | tf_op jit(solution)/shard_map/ppermute | solution.py:17
  29.7 4.2 %collective-permute-start.1 = (bf16[16,1,512]{2,1,0:T(2,128)(2,1)S(1)}, bf16[16,1,512]{2,1,0:T(2,128)(2,1)S(1)}, u32[]{:S(2)}, u32[]{:S(2)}) collective-permute-start(bf16[16,1,512]{2,1,0:T(2,128)(2,1)S(1)} %get-tuple-element.36), channel_id=1, source_target_pairs={{4,0},{8,4},{12,8},{5,1},{9,5},{13,9},{6,2},{10,6},{14,10},{7,3},{... | collective-permute-start | bytes 49160 | tf_op jit(solution)/shard_map/ppermute | solution.py:19
  35.2 7.1 %copy-start.5 = (f32[16,16]{1,0:T(8,128)S(1)}, f32[16,16]{1,0:T(8,128)}, u32[]{:S(2)}) copy-start(f32[16,16]{1,0:T(8,128)} %param.18) | copy-start | bytes 3076
  40.7 8.8 %copy-start.3 = (f32[4,16,2048]{2,1,0:T(8,128)S(1)}, f32[4,16,2048]{2,1,0:T(8,128)}, u32[]{:S(2)}) copy-start(f32[4,16,2048]{2,1,0:T(8,128)} %param.16) | copy-start | bytes 1572868
  44.3 20.0 %all-to-all-start.2 = ((f32[16,16,512]{2,1,0:T(8,128)}), f32[16,16,512]{2,1,0:T(8,128)S(1)}, u32[]{:S(2)}, u32[]{:S(2)}) async-start(f32[16,16,512]{2,1,0:T(8,128)} %copy.78), calls=%async_computation.2 | async-start | bytes 1048576 | tf_op jit(solution)/shard_map/all_to_all | solution.py:27
  64.3 12.3 %all-to-all-start.4 = ((f32[4,1,32768]{2,1,0:T(1,128)}), f32[4,1,32768]{2,1,0:T(1,128)S(1)}, u32[]{:S(2)}, u32[]{:S(2)}) async-start(f32[4,1,32768]{2,1,0:T(1,128)} %reshape.117), calls=%async_computation.4 | async-start | bytes 1048576 | tf_op jit(solution)/shard_map/all_to_all | solution.py:72
  76.6 25.4 %all-to-all-start.3 = ((f32[4,1,32768]{2,1,0:T(1,128)}), f32[4,1,32768]{2,1,0:T(1,128)S(1)}, u32[]{:S(2)}, u32[]{:S(2)}) async-start(f32[4,1,32768]{2,1,0:T(1,128)} %reshape.121), calls=%async_computation.3 | async-start | bytes 1048576 | tf_op jit(solution)/shard_map/all_to_all | solution.py:70
  134.9 17.8 %all-to-all-start.6 = ((f32[4,1,32768]{2,1,0:T(1,128)}), f32[4,1,32768]{2,1,0:T(1,128)S(1)}, u32[]{:S(2)}, u32[]{:S(2)}) async-start(f32[4,1,32768]{2,1,0:T(1,128)} %reshape.123), calls=%async_computation.6 | async-start | bytes 1048576 | tf_op jit(solution)/shard_map/all_to_all | solution.py:78
  169.3 24.7 %copy-start.1 = (f32[4,16,2048]{2,1,0:T(8,128)S(1)}, f32[4,16,2048]{2,1,0:T(8,128)}, u32[]{:S(2)}) copy-start(f32[4,16,2048]{2,1,0:T(8,128)} %param.14) | copy-start | bytes 1572868
  169.3 24.7 %copy-start.4 = (f32[4,16,2048]{2,1,0:T(8,128)S(1)}, f32[4,16,2048]{2,1,0:T(8,128)}, u32[]{:S(2)}) copy-start(f32[4,16,2048]{2,1,0:T(8,128)} %param.17) | copy-start | bytes 1572868
  171.0 2.7 %collective-permute-start.2 = (f32[16,1,512]{2,1,0:T(1,128)S(1)}, f32[16,1,512]{2,1,0:T(1,128)S(1)}, u32[]{:S(2)}, u32[]{:S(2)}) collective-permute-start(f32[16,1,512]{2,1,0:T(1,128)S(1)} %get-tuple-element.34), channel_id=1, source_target_pairs={{0,4},{4,8},{8,12},{1,5},{5,9},{9,13},{2,6},{6,10},{10,14},{3,7},{... | collective-permute-start | bytes 98312 | tf_op jit(solution)/shard_map/ppermute | solution.py:17
  172.4 4.2 %collective-permute-start.3 = (f32[16,1,512]{2,1,0:T(1,128)S(1)}, f32[16,1,512]{2,1,0:T(1,128)S(1)}, u32[]{:S(2)}, u32[]{:S(2)}) collective-permute-start(f32[16,1,512]{2,1,0:T(1,128)S(1)} %get-tuple-element.33), channel_id=1, source_target_pairs={{4,0},{8,4},{12,8},{5,1},{9,5},{13,9},{6,2},{10,6},{14,10},{7,3},{... | collective-permute-start | bytes 98312 | tf_op jit(solution)/shard_map/ppermute | solution.py:19
where the time goes:
time: 197 us; the launch traced here: 195 us
  local copies, waits for them, and re-layouts  81 us (41%)
  starting transfers between devices  32 us (16%)
  blocking collectives  29.1 us (15%)
  waiting for transfers between devices  25.7 us (13%)
  matrix products  15.3 us (8%)
  other arithmetic  10.8 us (5%)
    unnamed x28, local copies, waits for them, and re-layouts  53.2 us
    all_to_all x1, blocking collectives, to_frame_layout(): lax.all_to_all(blocked, 'frame', split_axis=0, concat_axis=2, tiled=True)  17.2 us
    all_to_all x1, waiting for transfers between devices, on_device(): lax.all_to_all(back_planes, 'frame', split_axis=2, concat_axis=0, tiled=T...  14.1 us
    all_to_all x1, blocking collectives, on_device(): lax.all_to_all(back_cols, 'zslab', split_axis=1, concat_axis=2, tiled=True)  11.9 us
    all_to_all x1, starting transfers between devices, on_device(): lax.all_to_all(lowered, 'frame', split_axis=2, concat_axis=0, tiled=True)  6.33 us
    all_to_all x1, waiting for transfers between devices, to_frame_layout(): lax.all_to_all(blocked, 'frame', split_axis=0, concat_axis=2, tiled=True)  6.05 us
    ppermute x2, waiting for transfers between devices, with_halo(): lax.ppermute(head, axis, [((i + 1) % count, i) for i in range(ends)])  5.56 us
    dot_general x1, matrix products, on_device(): jnp.einsum('smn,fsn->sfm', kernel, picked, preferred_element_type=jnp.flo...  5.47 us
  transfers between devices with their start and end apart: 10, of which 4 were waited for; matrix products, arithmetic and copies ran while one was open for 31% of the time, Pallas kernels for 0%

commit v1 on v0

v1 whole, which is shorter than its diff:
```python
import functools

import jax
import jax.numpy as jnp
from jax import lax
from jax.experimental import pallas as pl
from jax.experimental.pallas import tpu as pltpu
from jax.sharding import PartitionSpec as P

F32, BF16, I32 = jnp.float32, jnp.bfloat16, jnp.int32
MESH = pl.DeviceIdType.MESH
EXACT = lax.Precision.HIGHEST
REACH = 8
CHUNKS = 4
LEFT, RIGHT = 0, 1


def iota(shape, dim):
    return lax.broadcasted_iota(I32, shape, dim)


def hot(mask, dtype=F32):
    return jnp.where(mask, 1.0, 0.0).astype(dtype)


def exact(a, b):
    return jnp.dot(a, b, precision=EXACT, preferred_element_type=F32)


def exact_nt(a, b):
    return lax.dot_general(
        a, b, (((1,), (1,)), ((), ())), precision=EXACT, preferred_element_type=F32
    )


def em_kernel(
    sizes,
    alpha, measured, background, norm, temporal, axial, kernel,
    codes,
    out,
    outbox, inbox, image, coef, ratio, image_rim, coef_rim, ratio_rim, low, back,
    rim_out, rim, final_out, final_in, gathered,
    swap, forward_mix, backward_mix,
    a2a_send, a2a_recv, halo_send, halo_recv,
):
    ways, slabs, own, planes, tile, slots = sizes
    frames = ways * own
    width = tile // CHUNKS
    edge = 128
    per_chunk = width // edge
    tiles = tile // edge
    tiles_all = tiles * ways
    span = REACH * frames
    cells = planes * frames
    me = lax.axis_index("frame")
    slab = lax.axis_index("zslab")
    first = slab * planes
    beside = (lax.rem(slab + slabs - 1, slabs), lax.rem(slab + 1, slabs))

    def a2a(kind, c, o):
        if kind < 3:
            src, dst = outbox.at[kind, c, o - 1], inbox.at[kind, c, o]
        else:
            src, dst = final_out.at[c, o], final_in.at[c, o]
        return pltpu.make_async_remote_copy(
            src_ref=src, dst_ref=dst,
            send_sem=a2a_send.at[kind, c, o - 1], recv_sem=a2a_recv.at[kind, c, o - 1],
            device_id={"frame": lax.rem(me + o, ways)}, device_id_type=MESH,
        )

    def halo(kind, c, side):
        if kind == 0:
            src, dst = image.at[c, (1, planes)[side]], image_rim
        elif kind == 1:
            src, dst = coef.at[c, pl.ds((0, cells - span)[side], span)], coef_rim
        elif kind == 2:
            src, dst = ratio.at[c, pl.ds((0, cells - span)[side], span)], ratio_rim
        else:
            src, dst = rim_out.at[c, side], rim
        return pltpu.make_async_remote_copy(
            src_ref=src, dst_ref=dst.at[c, 1 - side],
            send_sem=halo_send.at[kind, c, side], recv_sem=halo_recv.at[kind, c, side],
            device_id={"zslab": beside[side]}, device_id_type=MESH,
        )

    def halo_start(kind, c):
        for side in (LEFT, RIGHT):
            halo(kind, c, side).start()

    def halo_wait(kind, c):
        for side in (LEFT, RIGHT):
            halo(kind, c, side).wait_recv()

    def fill(kind, source):
        for c in range(CHUNKS):
            for o in range(ways):
                lanes = pl.ds(pl.multiple_of(lax.rem(me + o, ways) * tile + c * width, edge), width)
                part = source[:, :, lanes].reshape(own * planes, width).astype(BF16)
                if o == 0:
                    inbox[kind, c, 0] = part
                else:
                    outbox[kind, c, o - 1] = part

    fill(0, alpha)
    fill(1, measured)
    fill(2, background)
    barrier = pltpu.get_barrier_semaphore()
    for o in range(1, ways):
        pl.semaphore_signal(
            barrier, inc=1, device_id={"frame": lax.rem(me + o, ways)}, device_id_type=MESH
        )
    for side in (LEFT, RIGHT):
        pl.semaphore_signal(
            barrier, inc=1, device_id={"zslab": beside[side]}, device_id_type=MESH
        )
    pl.semaphore_wait(barrier, ways + 1)
    for kinds in ((0,), (1, 2)):
        for c in range(CHUNKS):
            for kind in kinds:
                for o in range(1, ways):
                    a2a(kind, c, o).start()

    def frame_in(p):
        return lax.rem(me + ways - p // own, ways) * own + p % own

    def frame_out(p):
        return lax.rem(me + p // own, ways) * own + p % own

    row, column = iota((cells, cells), 0), iota((cells, cells), 1)
    swap[0] = hot(
        column % planes * frames + frame_in(column // planes) == row, BF16
    )
    swap[1] = hot(
        row % planes * frames + frame_out(row // planes) == column, BF16
    )

    def plane_at(k):
        return first + jnp.where(
            k < planes, k, jnp.where(k < planes + REACH, k - planes - REACH, k - REACH)
        )

    all_planes = axial.shape[0]
    wide = (planes + 2 * REACH) * frames
    halves = planes // REACH
    spread = hot(iota((all_planes, wide), 0) == plane_at(iota((all_planes, wide), 1) // frames))
    axial_wide = exact(axial[pl.ds(pl.multiple_of(first, REACH), planes), :], spread)
    time_wide = exact(temporal[...], hot(iota((frames, wide), 0) == iota((frames, wide), 1) % frames))
    time_rows = exact(
        hot(iota((span, frames), 1) == frame_in(iota((span, frames), 0) // REACH)), time_wide
    )
    for h in range(halves):
        axial_rows = jnp.broadcast_to(
            axial_wide[h * REACH:(h + 1) * REACH][None], (frames, REACH, wide)
        ).reshape(span, wide)
        forward_mix[h * span:(h + 1) * span] = (axial_rows * time_rows).astype(BF16)

    lane = iota((all_planes, wide), 1)
    spread = hot(
        iota((all_planes, wide), 0) == plane_at(lane // span * REACH + lane % REACH)
    )
    pick = hot(iota((planes, all_planes), 1) == first + iota((planes, all_planes), 0))
    axial_wide = exact(exact_nt(pick, axial[...]), spread)
    same = hot(iota((frames, frames), 0) == iota((frames, frames), 1))
    time_wide = exact(
        exact_nt(same, temporal[...]),
        hot(iota((frames, wide), 0) == frame_in(iota((frames, wide), 1) // REACH % frames)),
    )
    axial_rows = exact(hot(iota((cells, planes), 1) == iota((cells, planes), 0) // frames), axial_wide)
    time_rows = jnp.broadcast_to(time_wide[None], (planes, frames, wide)).reshape(cells, wide)
    backward_mix[...] = (axial_rows * time_rows).astype(BF16)

    def stage_image(c):
        for o in range(1, ways):
            a2a(0, c, o).wait_recv()
        moved = jnp.dot(swap[0], inbox[0, c].reshape(cells, width), preferred_element_type=F32)
        image[c, 1:planes + 1] = moved.astype(BF16).reshape(planes, frames, width)
        halo_start(0, c)

    group = 4

    def slot_of(r, j):
        return 3 * r + j, codes[3 * r + j]

    def weight(code, value):
        return jnp.where(code == value, 1.0, 0.0).astype(F32)

    def stage_forward(c):
        halo_wait(0, c)
        image[c, 0] = image_rim[c, LEFT]
        image[c, planes + 1] = image_rim[c, RIGHT]
        for b in range(per_chunk):
            lanes = slice(b * edge, (b + 1) * edge)

            def some_planes(step, carry):
                for u in range(group):
                    z = step * group + u
                    r = z * tiles + c * per_chunk + b
                    near = [image[c, z + d, :, lanes].astype(F32) for d in range(3)]
                    total = None
                    for j in range(3):
                        slot, code = slot_of(r, j)
                        picked = sum(near[d] * weight(code, d + 1) for d in range(3)).astype(BF16)
                        term = lax.dot_general(
                            picked, kernel[slot], (((1,), (1,)), ((), ())),
                            preferred_element_type=F32,
                        )
                        total = term if total is None else total + term
                    at = pl.multiple_of(z * frames, frames)
                    gathered[pl.ds(at, frames), lanes] = total.astype(BF16)
                return carry

            lax.fori_loop(0, planes // group, some_planes, 0)
        coef[c] = gathered[...]
        halo_start(1, c)

    def by_half(box, c, h):
        cube = box[c].astype(F32).reshape(frames, halves, REACH, width)
        return cube[:, h].reshape(span, width)

    def stage_ratio(c):
        for kind in (1, 2):
            for o in range(1, ways):
                a2a(kind, c, o).wait_recv()
        projected = jnp.dot(forward_mix[:, :cells], coef[c], preferred_element_type=F32)
        halo_wait(1, c)
        projected = projected + jnp.dot(
            forward_mix[:, cells:], coef_rim[c].reshape(2 * span, width), preferred_element_type=F32
        )
        for h in range(halves):
            expected = projected[h * span:(h + 1) * span] + by_half(inbox.at[2], c, h)
            ratio[c, h * span:(h + 1) * span] = (
                by_half(inbox.at[1], c, h) / expected
            ).astype(BF16)
        halo_start(2, c)

    def stage_back(c):
        mixed = jnp.dot(backward_mix[:, :cells], ratio[c], preferred_element_type=F32)
        halo_wait(2, c)
        mixed = mixed + jnp.dot(
            backward_mix[:, cells:], ratio_rim[c].reshape(2 * span, width), preferred_element_type=F32
        )
        low[c] = mixed.astype(BF16).reshape(planes, frames, width)
        back[c] = jnp.zeros((planes + 2, frames, width), F32)
        for b in range(per_chunk):
            lanes = slice(b * edge, (b + 1) * edge)

            def some_planes(step, carry):
                sums = [jnp.zeros((frames, edge), F32) for _ in range(group + 2)]
                for u in range(group):
                    z = step * group + u
                    r = z * tiles + c * per_chunk + b
                    values = low[c, z, :, lanes]
                    for j in range(3):
                        slot, code = slot_of(r, j)
                        term = jnp.dot(values, kernel[slot], preferred_element_type=F32)
                        for d in range(3):
                            sums[u + d] = sums[u + d] + term * weight(code, d + 1)
                for u in range(group + 2):
                    back[c, step * group + u, :, lanes] += sums[u]
                return carry

            lax.fori_loop(0, planes // group, some_planes, 0)
        rim_out[c, LEFT] = back[c, 0]
        rim_out[c, RIGHT] = back[c, planes + 1]
        halo_start(3, c)

    def stage_send(c):
        halo_wait(3, c)
        back[c, 1] += rim[c, 0]
        back[c, planes] += rim[c, 1]
        whole = back[c, 1:planes + 1].reshape(cells, width)
        high = whole.astype(BF16)
        rest = (whole - high.astype(F32)).astype(BF16)
        moved = jnp.dot(swap[1], high, preferred_element_type=F32) + jnp.dot(
            swap[1], rest, preferred_element_type=F32
        )
        moved = moved.reshape(ways, own * planes, width)
        final_out[c] = moved
        for o in range(1, ways):
            a2a(3, c, o).start()

    def stage_out(c):
        for o in range(ways):
            if o > 0:
                a2a(3, c, o).wait_recv()
            source = lax.rem(me + ways - o, ways)
            lanes = pl.ds(pl.multiple_of(source * tile + c * width, edge), width)
            values = (final_in if o else final_out)[c, o].reshape(own, planes, width)
            out[:, :, lanes] = alpha[:, :, lanes] * values / norm[:, :, lanes]

    stages = (stage_image, stage_forward, stage_ratio, stage_back, stage_send, stage_out)
    for t in range(CHUNKS + len(stages) - 1):
        for s, stage in enumerate(stages):
            if 0 <= t - s < CHUNKS:
                stage(t - s)

    for c in range(CHUNKS):
        for kind in range(4):
            for o in range(1, ways):
                a2a(kind, c, o).wait_send()
            for side in (LEFT, RIGHT):
                halo(kind, c, side).wait_send()


def on_device(alpha, measured, background, norm_image, temporal, axial, kernel, rows, cols, counts):
    own, planes, row_width = alpha.shape
    ways, slabs = lax.axis_size("frame"), lax.axis_size("zslab")
    slots, edge, _ = kernel.shape
    frames = ways * own
    tile = row_width // ways
    width = tile // CHUNKS
    cells = planes * frames
    wide = (planes + 2 * REACH) * frames
    tiles_all, tiles = row_width // edge, tile // edge
    first = lax.axis_index("zslab") * planes
    here = lax.axis_index("frame") * tiles
    local_rows = (rows // tiles_all - first) * tiles + rows % tiles_all - here
    step = cols // tiles_all - rows // tiles_all
    live = jnp.arange(slots, dtype=I32) < counts[0]
    local_rows = jnp.where(live, local_rows, planes * tiles)
    order = jnp.arange(planes * tiles, dtype=I32)
    starts = jnp.sum((local_rows[None, :] < order[:, None]).astype(I32), axis=1)
    places = starts[:, None] + jnp.arange(3, dtype=I32)[None, :]
    chosen = places[:, :, None] == jnp.arange(slots, dtype=I32)[None, None, :]
    mine = chosen & (local_rows[None, None, :] == order[:, None, None])
    codes = jnp.sum(jnp.where(mine, step + 2, 0), axis=2).reshape(-1)
    ordered = jnp.take(kernel, jnp.minimum(places, slots - 1).reshape(-1), axis=0, mode="clip")
    sizes = (ways, slabs, own, planes, tile, slots)
    vmem = pl.BlockSpec(memory_space=pltpu.VMEM)
    smem = pl.BlockSpec(memory_space=pltpu.SMEM)
    box = (CHUNKS, ways, own * planes, width)
    return pl.pallas_call(
        functools.partial(em_kernel, sizes),
        out_shape=jax.ShapeDtypeStruct(alpha.shape, F32),
        in_specs=[vmem] * 7 + [smem],
        out_specs=vmem,
        scratch_shapes=[
            pltpu.VMEM((3, CHUNKS, ways - 1, own * planes, width), BF16),
            pltpu.VMEM((3,) + box, BF16),
            pltpu.VMEM((CHUNKS, planes + 2, frames, width), BF16),
            pltpu.VMEM((CHUNKS, cells, width), BF16),
            pltpu.VMEM((CHUNKS, cells, width), BF16),
            pltpu.VMEM((CHUNKS, 2, frames, width), BF16),
            pltpu.VMEM((CHUNKS, 2, REACH * frames, width), BF16),
            pltpu.VMEM((CHUNKS, 2, REACH * frames, width), BF16),
            pltpu.VMEM((CHUNKS, planes, frames, width), BF16),
            pltpu.VMEM((CHUNKS, planes + 2, frames, width), F32),
            pltpu.VMEM((CHUNKS, 2, frames, width), F32),
            pltpu.VMEM((CHUNKS, 2, frames, width), F32),
            pltpu.VMEM(box, F32),
            pltpu.VMEM(box, F32),
            pltpu.VMEM((cells, width), BF16),
            pltpu.VMEM((2, cells, cells), BF16),
            pltpu.VMEM((cells, wide), BF16),
            pltpu.VMEM((cells, wide), BF16),
            pltpu.SemaphoreType.DMA((4, CHUNKS, ways - 1)),
            pltpu.SemaphoreType.DMA((4, CHUNKS, ways - 1)),
            pltpu.SemaphoreType.DMA((4, CHUNKS, 2)),
            pltpu.SemaphoreType.DMA((4, CHUNKS, 2)),
        ],
        compiler_params=pltpu.CompilerParams(
            collective_id=0, has_side_effects=True, vmem_limit_bytes=48 * 1024 * 1024
        ),
        cost_estimate=pl.CostEstimate(
            flops=8 * frames * slots * edge * edge, bytes_accessed=2 * slots * edge * edge,
            transcendentals=0,
        ),
    )(alpha, measured, background, norm_image, temporal, axial, ordered, codes)


def solution(mesh):
    placed = (
        P(("study", "frame"), "zslab", None),
        P(("study", "frame"), "zslab", None),
        P(("study", "frame"), "zslab", None),
        P(("study", "frame"), "zslab", None),
        P(),
        P(),
        P(("study", "zslab", "frame"), None, None),
        P(("study", "zslab", "frame")),
        P(("study", "zslab", "frame")),
        P(("study", "zslab", "frame")),
    )
    return jax.shard_map(
        on_device,
        mesh=mesh,
        in_specs=placed,
        out_specs=P(("study", "frame"), "zslab", None),
        check_vma=False,
    )
```

time: 197 us -> 59.5 us (0.30)
  local copies, waits for them, and re-layouts: 81 us -> 12.2 us
  Pallas kernels: 0 us -> 44.5 us
  starting transfers between devices: 32 us -> 0 us
  blocking collectives: 29.1 us -> 0 us
  waiting for transfers between devices: 25.7 us -> 0 us
  matrix products: 15.3 us -> 0 us
  other arithmetic: 10.8 us -> 1.85 us
    unnamed x28 -> x13, local copies, waits for them, and re-layouts: 53.2 us -> 0.83 us
    pallas_call x0 -> x1, Pallas kernels: none -> 44.5 us  [on_device(): pl.pallas_call(functools.partial(em_kernel, sizes), out_shape=jax.ShapeDt...]
    all_to_all x2 -> x0, blocking collectives: 29.1 us -> none  [the longest x1 17.2 us: to_frame_layout(): lax.all_to_all(blocked, 'frame', split_axis=0, concat_axis=2, tiled=True)]
    all_to_all x6 -> x0, starting transfers between devices: 25.8 us -> none  [the longest x1 6.33 us: on_device(): lax.all_to_all(lowered, 'frame', split_axis=2, concat_axis=0, tiled=True)]
    all_to_all x10 -> x0, local copies, waits for them, and re-layouts: 22 us -> none  [the longest x2 3.96 us: on_device(): lax.all_to_all(measured, 'zslab', split_axis=2, concat_axis=1, tiled=True)]
    all_to_all x6 -> x0, waiting for transfers between devices: 20.1 us -> none  [the longest x1 14.1 us: on_device(): lax.all_to_all(back_planes, 'frame', split_axis=2, concat_axis=0, tiled=T...]
    dot_general x8 -> x0, matrix products: 15.3 us -> none  [the longest x1 5.47 us: on_device(): jnp.einsum('smn,fsn->sfm', kernel, picked, preferred_element_type=jnp.flo...]
    gather x2 -> x1, local copies, waits for them, and re-layouts: 1.55 us -> 11 us  [on_device(): jnp.take(kernel, jnp.minimum(places, slots - 1).reshape(-1), axis=0, mode...]
  transfers between devices with their start and end apart: 10 -> 0, of which waited for: 4 -> 0; matrix products, arithmetic and copies ran while one was open for 31% -> 0% of each run, Pallas kernels for 0% -> 0%
where the time goes in v1:
time: 59.5 us; the launch traced here: 59.3 us
  Pallas kernels  44.5 us (75%)
  local copies, waits for them, and re-layouts  12.2 us (21%)
  other arithmetic  1.85 us (3%)
  between operations  0.76 us (1%)
    pallas_call x1, Pallas kernels, on_device(): pl.pallas_call(functools.partial(em_kernel, sizes), out_shape=jax.ShapeDt...  44.5 us
    gather x1, local copies, waits for them, and re-layouts, on_device(): jnp.take(kernel, jnp.minimum(places, slots - 1).reshape(-1), axis=0, mode...  11 us

profile of v1, /device:TPU:0, one launch (start us, length us, event | category | flops | bytes accessed | tf_op | source)
XLA Modules:
  0.0 59.3 jit_solution(15347514987146991382)
XLA Ops:
  0.7 0.7 %subtract_add_fusion = (s32[192]{0:T(256)S(1)}, s32[192]{0:T(256)S(1)}) fusion(s32[192]{0:T(256)} %param.18, s32[192]{0:T(256)} %param.17), kind=kLoop, calls=%fused_computation.21 | loop fusion | flops 6144 | bytes 3072 | tf_op jit(solution)/shard_map/add | solution.py:326
  1.4 0.7 %compare_select_fusion = s32[192]{0:T(256)S(1)} fusion(s32[192]{0:T(256)S(1)} %get-tuple-element.6, s32[]{:T(128)S(6)} %mul.12, s32[]{:T(128)S(6)} %mul.10, s32[]{:T(128)} %bitcast.1, s32[192]{0:T(256)} %param.17), kind=kLoop, calls=%fused_computation.13 | loop fusion | flops 3264 | bytes 2316 | tf_op jit(solution)/shard_map/jit(_where)/select_n | solution.py:320
  2.0 0.1 convert_reduce_fusion
  2.2 0.1 iota_add_fusion
  2.3 0.1 copy.11
  2.3 0.2 select_reduce_fusion
  2.6 0.1 reshape.77
  2.7 0.1 copy.12
  2.8 0.1 reshape.74.codes
  3.0 0.0 copy-start
  3.0 0.0 copy-start.1
  3.0 0.0 copy-start.2
  3.0 0.0 copy-start.3
  3.0 0.0 copy-start.4
  3.0 0.0 copy-start.5
  3.0 11.0 %gather_fusion = bf16[192,128,128]{2,1,0:T(8,128)(2,1)} fusion(bf16[192,128,128]{2,1,0:T(8,128)(2,1)} %param.16, s32[1024]{0:T(1024)S(1)} %pad_clamp_fusion), kind=kCustom, calls=%fused_computation | custom fusion | bytes 12583680 | tf_op jit(solution)/shard_map/jit(_take)/gather | solution.py:327
  14.0 0.0 copy-done
  14.0 0.0 copy-done.1
  14.0 0.0 copy-done.2
  14.0 0.0 copy-done.3
  14.0 0.0 copy-done.4
  14.0 0.0 copy-done.5
  14.1 44.5 %shard_map.100 = f32[4,16,2048]{2,1,0:T(8,128)S(1)} custom-call(f32[4,16,2048]{2,1,0:T(8,128)S(1)} %copy-done, f32[4,16,2048]{2,1,0:T(8,128)S(1)} %copy-done.1, f32[4,16,2048]{2,1,0:T(8,128)S(1)} %copy-done.2, f32[4,16,2048]{2,1,0:T(8,128)S(1)} %copy-done.3, f32[16,16]{1,0:T(8,128)S(1)} %copy-done.5, f32[64,64]{1,0:T(8,128)S(1)} %copy-done.4, ...), custom_call_target="tpu_custom_call" | custom-call | flops 402653184 | bytes 6291456 | tf_op jit(solution)/shard_map/pallas_call | solution.py:332
  58.5 0.8 %copy.15 = f32[4,16,2048]{2,1,0:T(8,128)} copy(f32[4,16,2048]{2,1,0:T(8,128)S(1)} %shard_map.100) | data formatting | bytes 1048576
  (2 shorter events, 0.0 us)
Async XLA Ops:
  3.0 11.0 %copy-start = (f32[4,16,2048]{2,1,0:T(8,128)S(1)}, f32[4,16,2048]{2,1,0:T(8,128)}, u32[]{:S(2)}) copy-start(f32[4,16,2048]{2,1,0:T(8,128)} %alpha.1) | copy-start | bytes 1572868
  3.0 11.0 %copy-start.1 = (f32[4,16,2048]{2,1,0:T(8,128)S(1)}, f32[4,16,2048]{2,1,0:T(8,128)}, u32[]{:S(2)}) copy-start(f32[4,16,2048]{2,1,0:T(8,128)} %measured.1) | copy-start | bytes 1572868
  3.0 11.0 %copy-start.2 = (f32[4,16,2048]{2,1,0:T(8,128)S(1)}, f32[4,16,2048]{2,1,0:T(8,128)}, u32[]{:S(2)}) copy-start(f32[4,16,2048]{2,1,0:T(8,128)} %background.1) | copy-start | bytes 1572868
  3.0 11.0 %copy-start.3 = (f32[4,16,2048]{2,1,0:T(8,128)S(1)}, f32[4,16,2048]{2,1,0:T(8,128)}, u32[]{:S(2)}) copy-start(f32[4,16,2048]{2,1,0:T(8,128)} %norm.1) | copy-start | bytes 1572868
  3.0 11.0 %copy-start.4 = (f32[64,64]{1,0:T(8,128)S(1)}, f32[64,64]{1,0:T(8,128)}, u32[]{:S(2)}) copy-start(f32[64,64]{1,0:T(8,128)} %axial.1) | copy-start | bytes 49156
  3.0 11.0 %copy-start.5 = (f32[16,16]{1,0:T(8,128)S(1)}, f32[16,16]{1,0:T(8,128)}, u32[]{:S(2)}) copy-start(f32[16,16]{1,0:T(8,128)} %temporal.1) | copy-start | bytes 3076

commit v2 on v1

--- a/solution.py
+++ b/solution.py
@@ -36,7 +36,7 @@
 def em_kernel(
     sizes,
     alpha, measured, background, norm, temporal, axial, kernel,
-    codes,
+    codes, chosen,
     out,
     outbox, inbox, image, coef, ratio, image_rim, coef_rim, ratio_rim, low, back,
     rim_out, rim, final_out, final_in, gathered,
@@ -179,7 +179,7 @@
     group = 4
 
     def slot_of(r, j):
-        return 3 * r + j, codes[3 * r + j]
+        return chosen[3 * r + j], codes[3 * r + j]
 
     def weight(code, value):
         return jnp.where(code == value, 1.0, 0.0).astype(F32)
@@ -324,7 +324,7 @@
     chosen = places[:, :, None] == jnp.arange(slots, dtype=I32)[None, None, :]
     mine = chosen & (local_rows[None, None, :] == order[:, None, None])
     codes = jnp.sum(jnp.where(mine, step + 2, 0), axis=2).reshape(-1)
-    ordered = jnp.take(kernel, jnp.minimum(places, slots - 1).reshape(-1), axis=0, mode="clip")
+    spots = jnp.minimum(places, slots - 1).reshape(-1)
     sizes = (ways, slabs, own, planes, tile, slots)
     vmem = pl.BlockSpec(memory_space=pltpu.VMEM)
     smem = pl.BlockSpec(memory_space=pltpu.SMEM)
@@ -332,7 +332,7 @@
     return pl.pallas_call(
         functools.partial(em_kernel, sizes),
         out_shape=jax.ShapeDtypeStruct(alpha.shape, F32),
-        in_specs=[vmem] * 7 + [smem],
+        in_specs=[vmem] * 7 + [smem] * 2,
         out_specs=vmem,
         scratch_shapes=[
             pltpu.VMEM((3, CHUNKS, ways - 1, own * planes, width), BF16),
@@ -365,7 +365,7 @@
             flops=8 * frames * slots * edge * edge, bytes_accessed=2 * slots * edge * edge,
             transcendentals=0,
         ),
-    )(alpha, measured, background, norm_image, temporal, axial, ordered, codes)
+    )(alpha, measured, background, norm_image, temporal, axial, kernel, codes, spots)
 
 
 def solution(mesh):

time: 59.5 us -> 54.3 us (0.913)
  local copies, waits for them, and re-layouts: 12.2 us -> 6.86 us
    gather x1 -> x0, local copies, waits for them, and re-layouts: 11 us -> none  [on_device(): jnp.take(kernel, jnp.minimum(places, slots - 1).reshape(-1), axis=0, mode...]
    unnamed x13, local copies, waits for them, and re-layouts: 0.83 us -> 6.41 us
where the time goes in v2:
time: 54.3 us; the launch traced here: 53.8 us
  Pallas kernels  44.4 us (82%)
  local copies, waits for them, and re-layouts  6.86 us (13%)
  other arithmetic  1.83 us (3%)
  between operations  0.69 us (1%)
    pallas_call x1, Pallas kernels, on_device(): pl.pallas_call(functools.partial(em_kernel, sizes), out_shape=jax.ShapeDt...  44.4 us
    unnamed x13, local copies, waits for them, and re-layouts  6.41 us

profile of v2, /device:TPU:0, one launch (start us, length us, event | category | flops | bytes accessed | tf_op | source)
XLA Modules:
  0.0 53.8 jit_solution(5677147194564253238)
XLA Ops:
  0.7 0.7 %compare_select_fusion = (s32[192]{0:T(256)S(1)}, s32[192]{0:T(256)S(1)}) fusion(s32[]{:T(128)S(6)} %mul.12, s32[]{:T(128)S(6)} %mul.10, s32[]{:T(128)} %bitcast.1, s32[192]{0:T(256)} %param.17), kind=kLoop, calls=%fused_computation.11 | loop fusion | flops 4800 | bytes 2316 | tf_op jit(solution)/shard_map/jit(_where)/select_n | solution.py:320
  1.3 0.7 %subtract_add_fusion = s32[192]{0:T(256)S(1)} fusion(s32[192]{0:T(256)S(1)} %get-tuple-element.6, s32[192]{0:T(256)} %param.18), kind=kLoop, calls=%fused_computation.19 | loop fusion | flops 3264 | bytes 2304 | tf_op jit(solution)/shard_map/add | solution.py:326
  2.0 0.1 convert_reduce_fusion
  2.2 0.1 broadcast_minimum_fusion
  2.2 0.1 min.12.chosen
  2.4 0.1 copy.11
  2.5 0.2 select_reduce_fusion
  2.7 0.1 copy.12
  2.8 0.1 reshape.52.codes
  3.0 0.0 copy-start
  3.0 1.0 %copy-done = f32[4,16,2048]{2,1,0:T(8,128)S(1)} copy-done((f32[4,16,2048]{2,1,0:T(8,128)S(1)}, f32[4,16,2048]{2,1,0:T(8,128)}, u32[]{:S(2)}) %copy-start) | copy-done | bytes 524312
  4.0 0.0 copy-start.1
  4.0 1.0 %copy-done.1 = f32[4,16,2048]{2,1,0:T(8,128)S(1)} copy-done((f32[4,16,2048]{2,1,0:T(8,128)S(1)}, f32[4,16,2048]{2,1,0:T(8,128)}, u32[]{:S(2)}) %copy-start.1) | copy-done | bytes 524312
  5.0 0.0 copy-start.2
  5.0 1.0 %copy-done.2 = f32[4,16,2048]{2,1,0:T(8,128)S(1)} copy-done((f32[4,16,2048]{2,1,0:T(8,128)S(1)}, f32[4,16,2048]{2,1,0:T(8,128)}, u32[]{:S(2)}) %copy-start.2) | copy-done | bytes 524312
  6.1 0.0 copy-start.3
  6.1 1.0 %copy-done.3 = f32[4,16,2048]{2,1,0:T(8,128)S(1)} copy-done((f32[4,16,2048]{2,1,0:T(8,128)S(1)}, f32[4,16,2048]{2,1,0:T(8,128)}, u32[]{:S(2)}) %copy-start.3) | copy-done | bytes 524312
  7.1 0.0 copy-start.4
  7.1 0.8 %copy-done.4 = f32[64,64]{1,0:T(8,128)S(1)} copy-done((f32[64,64]{1,0:T(8,128)S(1)}, f32[64,64]{1,0:T(8,128)}, u32[]{:S(2)}) %copy-start.4) | copy-done | bytes 16408
  7.9 0.0 copy-start.5
  7.9 0.7 %copy-done.5 = f32[16,16]{1,0:T(8,128)S(1)} copy-done((f32[16,16]{1,0:T(8,128)S(1)}, f32[16,16]{1,0:T(8,128)}, u32[]{:S(2)}) %copy-start.5) | copy-done | bytes 1048
  8.6 44.4 %shard_map.100 = f32[4,16,2048]{2,1,0:T(8,128)S(1)} custom-call(f32[4,16,2048]{2,1,0:T(8,128)S(1)} %copy-done, f32[4,16,2048]{2,1,0:T(8,128)S(1)} %copy-done.1, f32[4,16,2048]{2,1,0:T(8,128)S(1)} %copy-done.2, f32[4,16,2048]{2,1,0:T(8,128)S(1)} %copy-done.3, f32[16,16]{1,0:T(8,128)S(1)} %copy-done.5, f32[64,64]{1,0:T(8,128)S(1)} %copy-done.4, ...), custom_call_target="tpu_custom_call" | custom-call | flops 402653184 | bytes 6291456 | tf_op jit(solution)/shard_map/pallas_call | solution.py:332
  53.0 0.8 %copy.15 = f32[4,16,2048]{2,1,0:T(8,128)} copy(f32[4,16,2048]{2,1,0:T(8,128)S(1)} %shard_map.100) | data formatting | bytes 1048576
  (1 shorter events, 0.0 us)
Async XLA Ops:
  3.0 1.0 %copy-start = (f32[4,16,2048]{2,1,0:T(8,128)S(1)}, f32[4,16,2048]{2,1,0:T(8,128)}, u32[]{:S(2)}) copy-start(f32[4,16,2048]{2,1,0:T(8,128)} %alpha.1) | copy-start | bytes 1572868
  4.0 1.0 %copy-start.1 = (f32[4,16,2048]{2,1,0:T(8,128)S(1)}, f32[4,16,2048]{2,1,0:T(8,128)}, u32[]{:S(2)}) copy-start(f32[4,16,2048]{2,1,0:T(8,128)} %measured.1) | copy-start | bytes 1572868
  5.0 1.0 %copy-start.2 = (f32[4,16,2048]{2,1,0:T(8,128)S(1)}, f32[4,16,2048]{2,1,0:T(8,128)}, u32[]{:S(2)}) copy-start(f32[4,16,2048]{2,1,0:T(8,128)} %background.1) | copy-start | bytes 1572868
  6.1 1.0 %copy-start.3 = (f32[4,16,2048]{2,1,0:T(8,128)S(1)}, f32[4,16,2048]{2,1,0:T(8,128)}, u32[]{:S(2)}) copy-start(f32[4,16,2048]{2,1,0:T(8,128)} %norm.1) | copy-start | bytes 1572868
  7.1 0.8 %copy-start.4 = (f32[64,64]{1,0:T(8,128)S(1)}, f32[64,64]{1,0:T(8,128)}, u32[]{:S(2)}) copy-start(f32[64,64]{1,0:T(8,128)} %axial.1) | copy-start | bytes 49156
  7.9 0.7 %copy-start.5 = (f32[16,16]{1,0:T(8,128)S(1)}, f32[16,16]{1,0:T(8,128)}, u32[]{:S(2)}) copy-start(f32[16,16]{1,0:T(8,128)} %temporal.1) | copy-start | bytes 3076

commit v3 on v2

--- a/solution.py
+++ b/solution.py
@@ -35,13 +35,14 @@
 
 def em_kernel(
     sizes,
-    alpha, measured, background, norm, temporal, axial, kernel,
+    alpha_hbm, measured_hbm, background_hbm, norm_hbm, temporal, axial, kernel_hbm,
     codes, chosen,
     out,
+    alpha, measured, background, norm, kernel,
     outbox, inbox, image, coef, ratio, image_rim, coef_rim, ratio_rim, low, back,
     rim_out, rim, final_out, final_in, gathered,
     swap, forward_mix, backward_mix,
-    a2a_send, a2a_recv, halo_send, halo_recv,
+    a2a_send, a2a_recv, halo_send, halo_recv, local_sem,
 ):
     ways, slabs, own, planes, tile, slots = sizes
     frames = ways * own
@@ -101,9 +102,18 @@
                 else:
                     outbox[kind, c, o - 1] = part
 
-    fill(0, alpha)
-    fill(1, measured)
-    fill(2, background)
+    local = [
+        pltpu.make_async_copy(src, dst, local_sem.at[i])
+        for i, (src, dst) in enumerate(
+            ((alpha_hbm, alpha), (measured_hbm, measured), (background_hbm, background),
+             (kernel_hbm, kernel), (norm_hbm, norm))
+        )
+    ]
+    for copy in local:
+        copy.start()
+    for kind, source in enumerate((alpha, measured, background)):
+        local[kind].wait()
+        fill(kind, source)
     barrier = pltpu.get_barrier_semaphore()
     for o in range(1, ways):
         pl.semaphore_signal(
@@ -186,6 +196,8 @@
 
     def stage_forward(c):
         halo_wait(0, c)
+        if c == 0:
+            local[3].wait()
         image[c, 0] = image_rim[c, LEFT]
         image[c, planes + 1] = image_rim[c, RIGHT]
         for b in range(per_chunk):
@@ -280,6 +292,8 @@
             a2a(3, c, o).start()
 
     def stage_out(c):
+        if c == 0:
+            local[4].wait()
         for o in range(ways):
             if o > 0:
                 a2a(3, c, o).wait_recv()
@@ -326,15 +340,17 @@
     codes = jnp.sum(jnp.where(mine, step + 2, 0), axis=2).reshape(-1)
     spots = jnp.minimum(places, slots - 1).reshape(-1)
     sizes = (ways, slabs, own, planes, tile, slots)
+    hbm = pl.BlockSpec(memory_space=pl.ANY)
     vmem = pl.BlockSpec(memory_space=pltpu.VMEM)
     smem = pl.BlockSpec(memory_space=pltpu.SMEM)
     box = (CHUNKS, ways, own * planes, width)
     return pl.pallas_call(
         functools.partial(em_kernel, sizes),
         out_shape=jax.ShapeDtypeStruct(alpha.shape, F32),
-        in_specs=[vmem] * 7 + [smem] * 2,
+        in_specs=[hbm] * 4 + [vmem] * 2 + [hbm] + [smem] * 2,
         out_specs=vmem,
-        scratch_shapes=[
+        scratch_shapes=[pltpu.VMEM(alpha.shape, F32)] * 4 + [
+            pltpu.VMEM(kernel.shape, BF16),
             pltpu.VMEM((3, CHUNKS, ways - 1, own * planes, width), BF16),
             pltpu.VMEM((3,) + box, BF16),
             pltpu.VMEM((CHUNKS, planes + 2, frames, width), BF16),
@@ -357,6 +373,7 @@
             pltpu.SemaphoreType.DMA((4, CHUNKS, ways - 1)),
             pltpu.SemaphoreType.DMA((4, CHUNKS, 2)),
             pltpu.SemaphoreType.DMA((4, CHUNKS, 2)),
+            pltpu.SemaphoreType.DMA((5,)),
         ],
         compiler_params=pltpu.CompilerParams(
             collective_id=0, has_side_effects=True, vmem_limit_bytes=48 * 1024 * 1024

time: 54.3 us -> 52.2 us (0.961)
  Pallas kernels: 44.4 us -> 42.4 us
    pallas_call x1, Pallas kernels: 44.4 us -> 42.4 us  [on_device(): pl.pallas_call(functools.partial(em_kernel, sizes), out_shape=jax.ShapeDt...]
where the time goes in v3:
time: 52.2 us; the launch traced here: 51.8 us
  Pallas kernels  42.4 us (81%)
  local copies, waits for them, and re-layouts  6.86 us (13%)
  other arithmetic  1.83 us (4%)
  between operations  0.69 us (1%)
    pallas_call x1, Pallas kernels, on_device(): pl.pallas_call(functools.partial(em_kernel, sizes), out_shape=jax.ShapeDt...  42.4 us
    unnamed x13, local copies, waits for them, and re-layouts  6.41 us

profile of v3, /device:TPU:0, one launch (start us, length us, event | category | flops | bytes accessed | tf_op | source)
XLA Modules:
  0.0 51.8 jit_solution(8815957040284266993)
XLA Ops:
  0.7 0.7 %compare_select_fusion = (s32[192]{0:T(256)S(1)}, s32[192]{0:T(256)S(1)}) fusion(s32[]{:T(128)S(6)} %mul.12, s32[]{:T(128)S(6)} %mul.10, s32[]{:T(128)} %bitcast.1, s32[192]{0:T(256)} %param.17), kind=kLoop, calls=%fused_computation.11 | loop fusion | flops 4800 | bytes 2316 | tf_op jit(solution)/shard_map/jit(_where)/select_n | solution.py:334
  1.3 0.7 %subtract_add_fusion = s32[192]{0:T(256)S(1)} fusion(s32[192]{0:T(256)S(1)} %get-tuple-element.6, s32[192]{0:T(256)} %param.18), kind=kLoop, calls=%fused_computation.19 | loop fusion | flops 3264 | bytes 2304 | tf_op jit(solution)/shard_map/add | solution.py:340
  2.0 0.1 convert_reduce_fusion
  2.2 0.1 broadcast_minimum_fusion
  2.2 0.1 min.12.chosen
  2.4 0.1 copy.11
  2.5 0.2 select_reduce_fusion
  2.7 0.1 copy.12
  2.8 0.1 reshape.52.codes
  3.0 0.0 copy-start
  3.0 1.0 %copy-done = f32[4,16,2048]{2,1,0:T(8,128)S(1)} copy-done((f32[4,16,2048]{2,1,0:T(8,128)S(1)}, f32[4,16,2048]{2,1,0:T(8,128)}, u32[]{:S(2)}) %copy-start) | copy-done | bytes 524312
  4.0 0.0 copy-start.1
  4.0 1.0 %copy-done.1 = f32[4,16,2048]{2,1,0:T(8,128)S(1)} copy-done((f32[4,16,2048]{2,1,0:T(8,128)S(1)}, f32[4,16,2048]{2,1,0:T(8,128)}, u32[]{:S(2)}) %copy-start.1) | copy-done | bytes 524312
  5.0 0.0 copy-start.2
  5.0 1.0 %copy-done.2 = f32[4,16,2048]{2,1,0:T(8,128)S(1)} copy-done((f32[4,16,2048]{2,1,0:T(8,128)S(1)}, f32[4,16,2048]{2,1,0:T(8,128)}, u32[]{:S(2)}) %copy-start.2) | copy-done | bytes 524312
  6.1 0.0 copy-start.3
  6.1 1.0 %copy-done.3 = f32[4,16,2048]{2,1,0:T(8,128)S(1)} copy-done((f32[4,16,2048]{2,1,0:T(8,128)S(1)}, f32[4,16,2048]{2,1,0:T(8,128)}, u32[]{:S(2)}) %copy-start.3) | copy-done | bytes 524312
  7.1 0.0 copy-start.4
  7.1 0.8 %copy-done.4 = f32[64,64]{1,0:T(8,128)S(1)} copy-done((f32[64,64]{1,0:T(8,128)S(1)}, f32[64,64]{1,0:T(8,128)}, u32[]{:S(2)}) %copy-start.4) | copy-done | bytes 16408
  7.9 0.0 copy-start.5
  7.9 0.7 %copy-done.5 = f32[16,16]{1,0:T(8,128)S(1)} copy-done((f32[16,16]{1,0:T(8,128)S(1)}, f32[16,16]{1,0:T(8,128)}, u32[]{:S(2)}) %copy-start.5) | copy-done | bytes 1048
  8.6 42.4 %shard_map.100 = f32[4,16,2048]{2,1,0:T(8,128)S(1)} custom-call(f32[4,16,2048]{2,1,0:T(8,128)S(1)} %copy-done, f32[4,16,2048]{2,1,0:T(8,128)S(1)} %copy-done.1, f32[4,16,2048]{2,1,0:T(8,128)S(1)} %copy-done.2, f32[4,16,2048]{2,1,0:T(8,128)S(1)} %copy-done.3, f32[16,16]{1,0:T(8,128)S(1)} %copy-done.5, f32[64,64]{1,0:T(8,128)S(1)} %copy-done.4, ...), custom_call_target="tpu_custom_call" | custom-call | flops 402653184 | bytes 6291456 | tf_op jit(solution)/shard_map/pallas_call | solution.py:347
  51.0 0.8 %copy.15 = f32[4,16,2048]{2,1,0:T(8,128)} copy(f32[4,16,2048]{2,1,0:T(8,128)S(1)} %shard_map.100) | data formatting | bytes 1048576
  (1 shorter events, 0.0 us)
Async XLA Ops:
  3.0 1.0 %copy-start = (f32[4,16,2048]{2,1,0:T(8,128)S(1)}, f32[4,16,2048]{2,1,0:T(8,128)}, u32[]{:S(2)}) copy-start(f32[4,16,2048]{2,1,0:T(8,128)} %alpha_hbm.1) | copy-start | bytes 1572868
  4.0 1.0 %copy-start.1 = (f32[4,16,2048]{2,1,0:T(8,128)S(1)}, f32[4,16,2048]{2,1,0:T(8,128)}, u32[]{:S(2)}) copy-start(f32[4,16,2048]{2,1,0:T(8,128)} %measured_hbm.1) | copy-start | bytes 1572868
  5.0 1.0 %copy-start.2 = (f32[4,16,2048]{2,1,0:T(8,128)S(1)}, f32[4,16,2048]{2,1,0:T(8,128)}, u32[]{:S(2)}) copy-start(f32[4,16,2048]{2,1,0:T(8,128)} %background_hbm.1) | copy-start | bytes 1572868
  6.1 1.0 %copy-start.3 = (f32[4,16,2048]{2,1,0:T(8,128)S(1)}, f32[4,16,2048]{2,1,0:T(8,128)}, u32[]{:S(2)}) copy-start(f32[4,16,2048]{2,1,0:T(8,128)} %norm_hbm.1) | copy-start | bytes 1572868
  7.1 0.8 %copy-start.4 = (f32[64,64]{1,0:T(8,128)S(1)}, f32[64,64]{1,0:T(8,128)}, u32[]{:S(2)}) copy-start(f32[64,64]{1,0:T(8,128)} %axial.1) | copy-start | bytes 49156
  7.9 0.7 %copy-start.5 = (f32[16,16]{1,0:T(8,128)S(1)}, f32[16,16]{1,0:T(8,128)}, u32[]{:S(2)}) copy-start(f32[16,16]{1,0:T(8,128)} %temporal.1) | copy-start | bytes 3076
